TPU v7x, 256 devices: a whole 4x4x8 slice. The times are simulated.
256 devices in a mesh: grp: 16 (over x_hi, z), blk: 16 (over x_lo, y, core).
Axes of the slice: x: 4 (x_hi: 2, x_lo: 2; x = x_hi * 2 + x_lo), y: 4, z: 8, core: 2. Of those that a mesh axis runs over, the one named last changes fastest.
Arguments:
- prompt_of: int32 [2048], P(('grp', 'blk')), may hold values from 0 to 31, as said below
- suffix_len: int32 [2048], P(('grp', 'blk')), may hold values from 1 to 256, as said below
- query: bfloat16 [2048, 4096], P(('grp', 'blk')), may hold values from -8 to 23
- new_key: bfloat16 [2048, 512], P(('grp', 'blk')), may hold values from -5 to 6
- new_value: bfloat16 [2048, 512], P(('grp', 'blk')), may hold values from -6 to 6
- suffix_key: bfloat16 [2048, 256, 512], P(('grp', 'blk')), may hold values from -5 to 6
- suffix_value: bfloat16 [2048, 256, 512], P(('grp', 'blk')), may hold values from -6 to 6
- prefix_key: bfloat16 [32, 4096, 512], P('grp', 'blk'), may hold values from -5 to 6
- prefix_value: bfloat16 [32, 4096, 512], P('grp', 'blk'), may hold values from -6 to 6
Outputs:
- attended: bfloat16 [2048, 4096], P(('grp', 'blk'))
Inputs may be any that keep to these rules, and one draw needn't show every extreme that they name: `prompt_of`: on every device at most 2 of its completions name prompts of one group (the group of a prompt is prompt // 2); one group gets exactly 2 from every device. `suffix_len`: some completion has exactly 256 cached suffix tokens.
All inputs are finite; a program needn't handle non-finite values.
Results may differ from a plain program's by a relative error of at most 0.0037.
Values may be sent and summed in bfloat16 or wider, within the bound.
No kernel may reach another device: no remote copies, remote signals or barrier semaphores. Data moves between devices by JAX's collectives and lax.ppermute only.
A program may use at most 128 MiB of HBM per device.

v0:
```python
import math

import jax
import jax.numpy as jnp
from jax import lax
from jax.experimental import pallas as pl
from jax.experimental.pallas import tpu as pltpu
from jax.sharding import Mesh, PartitionSpec as P

HD = 128
CAP = 2
HELD = 8
HEADS = 32
KVH = 4
RATIO = 8
PROMPTS = 32
SUF = 256
PIECE = 256
SLOTS = 256
ROWS = SLOTS * RATIO
NEG = -1e30
SCALE = HD ** (-0.5)
LOG2E = 1.4426950408889634
ALL = ("xh", "z", "xl", "y", "c")
NEAR = ("xl", "y")
FAR = ("xh", "z", "xl")


def slots_of(prompt_ref):
    prompts = [prompt_ref[i] for i in range(HELD)]
    slots = []
    for i in range(HELD):
        rank = jnp.int32(0)
        for j in range(i):
            rank = rank + jnp.where(prompts[j] == prompts[i], 1, 0)
        slots.append(prompts[i] * CAP + rank)
    return slots


def spread(values, index):
    picked = jnp.zeros(index.shape, jnp.int32)
    for i, value in enumerate(values):
        picked = jnp.where(index == i, value, picked)
    return picked


def prep_kernel(place_ref, prompt_hbm, query_hbm, key_ref, value_ref, send_ref, *refs):
    cut_refs = refs[:8]
    prompt_ref, query_ref, small_sem, cut_sem = refs[8:]
    small = [
        pltpu.make_async_copy(prompt_hbm, prompt_ref, small_sem.at[0]),
        pltpu.make_async_copy(query_hbm, query_ref, small_sem.at[1]),
    ]
    for copy in small:
        copy.start()
    place = place_ref[0]
    copies = []
    for step, cut_ref in enumerate(cut_refs):
        target = place ^ step
        prompt = target >> 2
        column = pl.multiple_of((target & 3) * HD, HD)
        for n, cache in enumerate((key_ref, value_ref)):
            copies.append(
                pltpu.make_async_copy(
                    cache.at[prompt, :, pl.ds(column, HD)], cut_ref.at[n], cut_sem.at[step, n]
                )
            )
            copies[-1].start()
    for copy in small:
        copy.wait()
    slots = slots_of(prompt_ref)
    lane = lax.broadcasted_iota(jnp.int32, (HELD, HD), 1)
    row = lax.broadcasted_iota(jnp.int32, (HELD, HD), 0)
    tags = jnp.concatenate(
        [spread(slots, lane & 7).astype(jnp.float32), spread(slots, row).astype(jnp.float32)], axis=0
    ).astype(jnp.bfloat16)
    for y in range(KVH):
        send_ref[y, :64] = jnp.concatenate(
            [
                query_ref[:, h * HD : (h + 1) * HD].astype(jnp.float32)
                for h in range(y * RATIO, (y + 1) * RATIO)
            ],
            axis=0,
        ).astype(jnp.bfloat16)
        send_ref[y, 64:] = tags
    for copy in copies:
        copy.wait()


def pack_kernel(got_ref, *refs):
    out_ref = refs[-1]
    held = got_ref[:, :64].reshape(256, HD)
    tags = [got_ref[y, 64:].astype(jnp.float32)[:1].astype(jnp.int32) for y in range(KVH)]
    half = lax.broadcasted_iota(jnp.int32, (1, HD), 1) < 64
    tag = jnp.concatenate([jnp.where(half, tags[0], tags[1]), jnp.where(half, tags[2], tags[3])], axis=1)
    lane_key = (lax.broadcasted_iota(jnp.int32, (1, 256), 1) >> 3) * 64 + tag
    chunk = 512
    for start in range(0, ROWS, chunk):
        row = lax.broadcasted_iota(jnp.int32, (chunk, 1), 0) + start
        row_key = ((row >> 1) & 3) * 512 + ((row >> 3) & 7) * 64 + (row >> 6) * 2 + (row & 1)
        select = (row_key == lane_key).astype(jnp.float32).astype(jnp.bfloat16)
        out_ref[start : start + chunk, :] = jnp.dot(
            select, held, preferred_element_type=jnp.float32
        ).astype(jnp.bfloat16)


def near_kernel(
    len_ref, query_ref, new_key_ref, new_value_ref, key_ref, value_ref, out_ref, lse_ref, heads_ref
):
    step = pl.program_id(0)

    @pl.when(step == 0)
    def _():
        for h in range(HEADS):
            heads_ref[h] = query_ref[:, h * HD : (h + 1) * HD].astype(jnp.float32)

    length = len_ref[step]
    query = heads_ref[:, pl.ds(step, 1), :].reshape(HEADS, HD)
    keys = key_ref[0]
    values = value_ref[0]
    held_row = lax.broadcasted_iota(jnp.int32, (HELD, 1), 0)

    def row_of(ref):
        rows = jnp.where(held_row == step, ref[...].astype(jnp.float32), 0.0)
        return jnp.sum(rows, axis=0, keepdims=True)

    new_key = row_of(new_key_ref)
    new_value = row_of(new_value_ref)

    def spread_heads(row):
        return jnp.concatenate(
            [jnp.broadcast_to(row[:, k * HD : (k + 1) * HD], (RATIO, HD)) for k in range(KVH)], axis=0
        )

    scores = jnp.concatenate(
        [
            lax.dot_general(
                query.astype(jnp.bfloat16),
                keys[:, k * HD : (k + 1) * HD],
                (((1,), (1,)), ((), ())),
                preferred_element_type=jnp.float32,
            )[k * RATIO : (k + 1) * RATIO]
            for k in range(KVH)
        ],
        axis=0,
    ) * SCALE
    own = jnp.sum(query * spread_heads(new_key), axis=1, keepdims=True) * SCALE
    live = lax.broadcasted_iota(jnp.int32, (1, SUF), 1) < length
    scores = jnp.where(live, scores, NEG)
    top = jnp.maximum(jnp.max(scores, axis=1, keepdims=True), own)
    weights = jnp.where(live, jnp.exp(scores - top), 0.0)
    own_weight = jnp.exp(own - top)
    total = jnp.sum(weights, axis=1, keepdims=True) + own_weight
    rounded = weights.astype(jnp.bfloat16)
    mixed = jnp.concatenate(
        [
            jnp.dot(rounded, values[:, k * HD : (k + 1) * HD], preferred_element_type=jnp.float32)[
                k * RATIO : (k + 1) * RATIO
            ]
            for k in range(KVH)
        ],
        axis=0,
    )
    mixed = mixed + own_weight.astype(jnp.bfloat16).astype(jnp.float32) * spread_heads(new_value)
    out_ref[:, pl.ds(step, 1), :] = (mixed / total).reshape(HEADS, 1, HD)
    lse_ref[:, pl.ds(step, 1), :] = jnp.broadcast_to(top + jnp.log(total), (HEADS, HD)).reshape(
        HEADS, 1, HD
    )


def far_kernel(query_ref, *refs):
    sources = refs[:16]
    out_ref, score_ref, query_scr, mixed_scr, stat_scr, cache_ref, sems = refs[16:]
    copies = [
        pltpu.make_async_copy(source, cache_ref.at[n], sems.at[n]) for n, source in enumerate(sources)
    ]
    for copy in copies:
        copy.start()
    pieces = [cache_ref.at[n] for n in range(16)]
    span = 32
    block = span * RATIO
    tokens = 16 * PIECE
    queries = query_ref[...].astype(jnp.float32).reshape(32, RATIO, 8, HD)
    biggest = jnp.max(jnp.max(jnp.abs(queries), axis=1).reshape(SLOTS, HD), axis=1, keepdims=True)
    valid = (biggest > 0).astype(jnp.float32)
    row = lax.broadcasted_iota(jnp.int32, (SLOTS, SLOTS), 0)
    lane = lax.broadcasted_iota(jnp.int32, (SLOTS, SLOTS), 1)
    wide = jnp.broadcast_to(valid, (SLOTS, SLOTS)).astype(jnp.bfloat16)
    before = jnp.dot(
        (lane < row).astype(jnp.float32).astype(jnp.bfloat16), wide, preferred_element_type=jnp.float32
    )
    order = jnp.where(valid > 0, before, -1.0).astype(jnp.int32)
    gather = (order == lane).astype(jnp.float32).astype(jnp.bfloat16)
    count = jnp.sum(valid).astype(jnp.int32)
    for h in range(RATIO):
        query_scr[h] = lax.dot_general(
            gather,
            queries[:, h].reshape(SLOTS, HD).astype(jnp.bfloat16),
            (((0,), (0,)), ((), ())),
            preferred_element_type=jnp.float32,
        ).astype(jnp.bfloat16)
    mixed_scr[...] = jnp.zeros_like(mixed_scr)
    stat_scr[...] = jnp.zeros_like(stat_scr)
    for copy in copies:
        copy.wait()

    @pl.loop(0, (count + span - 1) // span)
    def _(index):
        start = pl.multiple_of(index * span, span)
        query = query_scr[:, pl.ds(start, span), :].reshape(block, HD)
        peak = jnp.full((block, HD), -jnp.inf, jnp.float32)
        for n, piece in enumerate(pieces):
            scores = lax.dot_general(
                query, piece[0], (((1,), (1,)), ((), ())), preferred_element_type=jnp.float32
            )
            score_ref[n] = scores
            peak = jnp.maximum(peak, jnp.maximum(scores[:, :HD], scores[:, HD:]))
        peak = jnp.max(peak, axis=1, keepdims=True)
        total = jnp.zeros((block, HD), jnp.float32)
        mixed = jnp.zeros((block, HD), jnp.float32)
        for n, piece in enumerate(pieces):
            weights = jnp.exp2((score_ref[n] - peak) * (SCALE * LOG2E))
            total = total + (weights[:, :HD] + weights[:, HD:])
            mixed = mixed + jnp.dot(
                weights.astype(jnp.bfloat16), piece[1], preferred_element_type=jnp.float32
            )
        total = jnp.sum(total, axis=1, keepdims=True)
        mixed_scr[:, pl.ds(start, span), :] = (mixed / total).astype(jnp.bfloat16).reshape(RATIO, span, HD)
        lse = peak * SCALE + jnp.log(total)
        stat_scr[pl.ds(start, span), :] = split_stat(lse.reshape(RATIO, span, 1), span).astype(jnp.bfloat16)

    idle = 1.0 - valid
    mean = sum(piece[1].astype(jnp.float32).reshape(PIECE // 8, 8, HD).sum(axis=0) for piece in pieces)
    mean = jnp.sum(mean, axis=0, keepdims=True) / tokens
    heads = []
    for h in range(RATIO):
        spread_out = jnp.dot(gather, mixed_scr[h], preferred_element_type=jnp.float32) + idle * mean
        heads.append(spread_out.reshape(32, 8, HD))
    for h in range(0, RATIO, 2):
        out_ref[:, h * 8 : h * 8 + 16] = jnp.concatenate(heads[h : h + 2], axis=1).astype(jnp.bfloat16)
    even = split_stat(jnp.full((RATIO, SLOTS, 1), math.log(tokens), jnp.float32), SLOTS)
    stat = jnp.dot(gather, stat_scr[...], preferred_element_type=jnp.float32) + idle * even
    stat = stat.reshape(32, 8, HD)
    out_ref[:, 64:] = jnp.concatenate([stat, jnp.zeros_like(stat)], axis=1).astype(jnp.bfloat16)


def split_stat(lse, span):
    high = lse.astype(jnp.bfloat16).astype(jnp.float32)
    rest = lse - high
    middle = rest.astype(jnp.bfloat16).astype(jnp.float32)
    low = rest - middle
    lane = lax.broadcasted_iota(jnp.int32, (span, HD), 1)
    stat = jnp.zeros((span, HD), jnp.float32)
    for h in range(RATIO):
        for n, part in enumerate((high, middle, low)):
            stat = jnp.where(lane == n * 8 + h, part[h], stat)
    return stat


def select_kernel(got_ref, back_ref, *refs):
    send_ref = refs[-1]
    tags = [got_ref[y, 64:].astype(jnp.float32)[8:, :1].astype(jnp.int32) for y in range(KVH)]
    lane = lax.broadcasted_iota(jnp.int32, (1, ROWS), 1)
    lane_key = ((lane >> 1) & 3) * 512 + ((lane >> 3) & 7) * 64 + (lane >> 6) * 2 + (lane & 1)
    tag = jnp.concatenate([tags[y] for y in range(KVH) for _ in range(RATIO)], axis=0)
    row_key = (lax.broadcasted_iota(jnp.int32, (256, 1), 0) >> 3) * 64 + tag
    select = (row_key == lane_key).astype(jnp.float32).astype(jnp.bfloat16)
    far = jnp.dot(select, back_ref[:, :64].reshape(ROWS, HD), preferred_element_type=jnp.float32)
    send_ref[:, :64] = far.astype(jnp.bfloat16).reshape(KVH, 64, HD)
    stats = back_ref[:, 64:].astype(jnp.float32)[:, :8].reshape(SLOTS, HD).astype(jnp.bfloat16)
    lane = lax.broadcasted_iota(jnp.int32, (1, SLOTS), 1)
    lane_key = ((lane >> 1) & 3) * 64 + (lane >> 3) * 2 + (lane & 1)
    row_key = (lax.broadcasted_iota(jnp.int32, (32, 1), 0) >> 3) * 64 + jnp.concatenate(tags, axis=0)
    select = (row_key == lane_key).astype(jnp.float32).astype(jnp.bfloat16)
    stat = jnp.dot(select, stats, preferred_element_type=jnp.float32).reshape(KVH, 8, HD)
    send_ref[:, 64:] = jnp.concatenate([stat, jnp.zeros_like(stat)], axis=1).astype(jnp.bfloat16)


def merge_kernel(back_ref, near_ref, near_lse_ref, out_ref):
    lane = lax.broadcasted_iota(jnp.int32, (HELD, HD), 1)
    for y in range(KVH):
        far = back_ref[y, :64].astype(jnp.float32)
        stat = jnp.where(lane < 24, back_ref[y, 64:].astype(jnp.float32)[:8], 0.0)
        for h in range(RATIO):
            head = y * RATIO + h
            far_lse = jnp.sum(jnp.where((lane & 7) == h, stat, 0.0), axis=1, keepdims=True)
            near_lse = near_lse_ref[head]
            top = jnp.maximum(far_lse, near_lse)
            far_scale = jnp.exp(far_lse - top)
            near_scale = jnp.exp(near_lse - top)
            merged = far[h * 8 : (h + 1) * 8] * far_scale + near_ref[head] * near_scale
            out_ref[:, head * HD : (head + 1) * HD] = (merged / (far_scale + near_scale)).astype(
                jnp.bfloat16
            )


VMEM = pl.BlockSpec(memory_space=pltpu.VMEM)
SMEM = pl.BlockSpec(memory_space=pltpu.SMEM)
ANY = pl.BlockSpec(memory_space=pl.ANY)
HBM = pl.BlockSpec(memory_space=pltpu.HBM)


def params(mib):
    return pltpu.CompilerParams(vmem_limit_bytes=mib << 20)


def shards(
    prompt_of,
    suffix_len,
    query,
    new_key,
    new_value,
    suffix_key,
    suffix_value,
    prefix_key,
    prefix_value,
):
    place = lax.axis_index(NEAR).astype(jnp.int32).reshape(1)
    sent, *cuts = pl.pallas_call(
        prep_kernel,
        out_shape=[jax.ShapeDtypeStruct((KVH, 80, HD), jnp.bfloat16)]
        + [jax.ShapeDtypeStruct((2, PIECE, HD), jnp.bfloat16)] * 8,
        in_specs=[SMEM, HBM, HBM, HBM, HBM],
        out_specs=[VMEM] * 9,
        scratch_shapes=[
            pltpu.SMEM((HELD,), jnp.int32),
            pltpu.VMEM((HELD, HEADS * HD), jnp.bfloat16),
            pltpu.SemaphoreType.DMA((2,)),
            pltpu.SemaphoreType.DMA((8, 2)),
        ],
        compiler_params=params(12),
        name="prep",
    )(place, prompt_of, query, prefix_key, prefix_value)
    held = [cuts[0]]
    for step in range(1, 8):
        held.append(lax.ppermute(cuts[step], NEAR, [(i, i ^ step) for i in range(8)]))
    swapped = [lax.ppermute(piece, "c", [(0, 1), (1, 0)]) for piece in held]
    got = lax.all_to_all(sent, "y", 0, 0, tiled=True)
    outgoing = pl.pallas_call(
        pack_kernel,
        out_shape=jax.ShapeDtypeStruct((ROWS, HD), jnp.bfloat16),
        in_specs=[VMEM] + [ANY] * 4,
        out_specs=VMEM,
        compiler_params=params(8),
        name="pack",
    )(got, *held[4:])
    arrived = lax.all_to_all(outgoing.reshape(PROMPTS, 64, HD), FAR, 0, 0, tiled=True)

    near_out, near_lse = pl.pallas_call(
        near_kernel,
        grid=(HELD,),
        out_shape=[jax.ShapeDtypeStruct((HEADS, HELD, HD), jnp.float32)] * 2,
        in_specs=[
            SMEM,
            pl.BlockSpec((HELD, HEADS * HD), lambda i: (0, 0)),
            pl.BlockSpec((HELD, KVH * HD), lambda i: (0, 0)),
            pl.BlockSpec((HELD, KVH * HD), lambda i: (0, 0)),
            pl.BlockSpec((1, SUF, KVH * HD), lambda i: (i, 0, 0)),
            pl.BlockSpec((1, SUF, KVH * HD), lambda i: (i, 0, 0)),
        ],
        out_specs=[pl.BlockSpec((HEADS, HELD, HD), lambda i: (0, 0, 0))] * 2,
        scratch_shapes=[pltpu.VMEM((HEADS, HELD, HD), jnp.float32)],
        compiler_params=params(12),
        cost_estimate=pl.CostEstimate(flops=300_000_000, bytes_accessed=4_500_000, transcendentals=65536),
        name="near",
    )(
        suffix_len,
        query,
        new_key,
        new_value,
        suffix_key,
        suffix_value,
    )

    parcel = pl.pallas_call(
        far_kernel,
        out_shape=jax.ShapeDtypeStruct((PROMPTS, 80, HD), jnp.bfloat16),
        in_specs=[VMEM] + [ANY] * 16,
        out_specs=VMEM,
        scratch_shapes=[
            pltpu.VMEM((16, 256, PIECE), jnp.float32),
            pltpu.VMEM((RATIO, SLOTS, HD), jnp.bfloat16),
            pltpu.VMEM((RATIO, SLOTS, HD), jnp.bfloat16),
            pltpu.VMEM((SLOTS, HD), jnp.bfloat16),
            pltpu.VMEM((16, 2, PIECE, HD), jnp.bfloat16),
            pltpu.SemaphoreType.DMA((16,)),
        ],
        compiler_params=params(60),
        name="far",
    )(arrived.reshape(ROWS, HD), *held, *swapped)
    back = lax.all_to_all(parcel, FAR, 0, 0, tiled=True)
    chosen = pl.pallas_call(
        select_kernel,
        out_shape=jax.ShapeDtypeStruct((KVH, 80, HD), jnp.bfloat16),
        in_specs=[VMEM] * 2 + [ANY] * 2,
        out_specs=VMEM,
        compiler_params=params(8),
        name="select",
    )(got, back, near_out, near_lse)
    final = lax.all_to_all(chosen, "y", 0, 0, tiled=True)
    return pl.pallas_call(
        merge_kernel,
        out_shape=jax.ShapeDtypeStruct((HELD, HEADS * HD), jnp.bfloat16),
        in_specs=[VMEM] * 3,
        out_specs=VMEM,
        compiler_params=params(12),
        name="merge",
    )(final, near_out, near_lse)


def solution(mesh):
    fine = Mesh(mesh.devices.reshape(2, 8, 2, 4, 2), ALL)
    grp = ("xh", "z")
    blk = ("xl", "y", "c")
    in_specs = (
        P(ALL),
        P(ALL),
        P(ALL, None),
        P(ALL, None),
        P(ALL, None),
        P(ALL, None, None),
        P(ALL, None, None),
        P(grp, blk, None),
        P(grp, blk, None),
    )
    return jax.shard_map(
        shards, mesh=fine, in_specs=in_specs, out_specs=P(ALL, None), check_vma=False
    )
```

profile of v0, /device:TPU:32, one launch (start us, length us, event | category | flops | bytes accessed | tf_op | source)
XLA Modules:
  0.0 99.4 jit_solution(17189435765072904139)
XLA Ops:
  0.0 1.0 %copy-done.6 = bf16[2,256,512]{2,1,0:T(8,128)(2,1)S(1)} copy-done((bf16[2,256,512]{2,1,0:T(8,128)(2,1)S(1)}, bf16[2,256,512]{2,1,0:T(8,128)(2,1)}, u32[]{:S(2)}) %copy-start.6) | copy-done | bytes 524312
  1.0 1.0 %copy-done.7 = bf16[2,256,512]{2,1,0:T(8,128)(2,1)S(1)} copy-done((bf16[2,256,512]{2,1,0:T(8,128)(2,1)S(1)}, bf16[2,256,512]{2,1,0:T(8,128)(2,1)}, u32[]{:S(2)}) %copy-start.7) | copy-done | bytes 524312
  2.1 0.8 copy-done.8
  2.9 0.7 copy-done.13
  3.6 0.8 prep.1
  4.4 1.6 %collective-permute-start = (bf16[2,256,128]{2,1,0:T(8,128)(2,1)S(1)}, bf16[2,256,128]{2,1,0:T(8,128)(2,1)S(1)}, u32[]{:S(2)}, u32[]{:S(2)}) collective-permute-start(bf16[2,256,128]{2,1,0:T(8,128)(2,1)S(1)} %get-tuple-element.17), channel_id=1, source_target_pairs={{0,8},{2,10},{4,12},{6,14},{8,0},{10,2},{12,4},{14,6},{1,9},{3,11}... | collective-permute-start | bytes 393224 | tf_op jit(solution)/shard_map/ppermute | solution.py:336
  5.9 1.5 %collective-permute-start.1 = (bf16[2,256,128]{2,1,0:T(8,128)(2,1)S(1)}, bf16[2,256,128]{2,1,0:T(8,128)(2,1)S(1)}, u32[]{:S(2)}, u32[]{:S(2)}) collective-permute-start(bf16[2,256,128]{2,1,0:T(8,128)(2,1)S(1)} %get-tuple-element.18), channel_id=1, source_target_pairs={{0,10},{2,8},{4,14},{6,12},{8,2},{10,0},{12,6},{14,4},{1,11},{3,9}... | collective-permute-start | bytes 393224 | tf_op jit(solution)/shard_map/ppermute | solution.py:336
  7.5 3.8 %collective-permute-start.2 = (bf16[2,256,128]{2,1,0:T(8,128)(2,1)S(1)}, bf16[2,256,128]{2,1,0:T(8,128)(2,1)S(1)}, u32[]{:S(2)}, u32[]{:S(2)}) collective-permute-start(bf16[2,256,128]{2,1,0:T(8,128)(2,1)S(1)} %get-tuple-element.19), channel_id=1, source_target_pairs={{0,12},{2,14},{4,8},{6,10},{8,4},{10,6},{12,0},{14,2},{1,13},{3,15... | collective-permute-start | bytes 393224 | tf_op jit(solution)/shard_map/ppermute | solution.py:336
  11.5 10.1 %all_to_all.20.got_ref = bf16[4,80,128]{2,1,0:T(8,128)(2,1)S(1)} all-to-all(bf16[4,80,128]{2,1,0:T(8,128)(2,1)S(1)} %get-tuple-element.16), channel_id=1, replica_groups=mesh['xh'=2,'z'=8,'xl'=2,'y'=4,'c'=2] {'y'}, dimensions={0} | all-to-all | bytes 163840 | tf_op jit(solution)/shard_map/all_to_all | solution.py:338
  21.7 1.5 %pack.1 = bf16[2048,128]{1,0:T(8,128)(2,1)} custom-call(bf16[4,80,128]{2,1,0:T(8,128)(2,1)S(1)} %all_to_all.20.got_ref, bf16[2,256,128]{2,1,0:T(8,128)(2,1)S(1)} %collective-permute-done.refs_0_.refs_4_, bf16[2,256,128]{2,1,0:T(8,128)(2,1)S(1)} %collective-permute-done.1.refs_1_.refs_5_, bf16[2,256,128]{2,1,0:T(8,128)(2,1)S(1)} %collective-permute-done.2.refs_2_.refs_6_, ...), custom_call_target="tpu_custom_call" | custom-call | tf_op jit(solution)/shard_map/pack/pallas_call | solution.py:339
  23.2 11.2 %all-to-all-start.1 = ((bf16[32,64,128]{2,1,0:T(8,128)(2,1)}), bf16[32,64,128]{2,1,0:T(8,128)(2,1)S(1)}, u32[]{:S(2)}, u32[]{:S(2)}) async-start(bf16[32,64,128]{2,1,0:T(8,128)(2,1)} %bitcast.1), calls=%async_computation.1 | async-start | bytes 1048576 | tf_op jit(solution)/shard_map/all_to_all | solution.py:347
  34.4 1.0 collective-permute-start.6
  35.4 3.8 %collective-permute-start.5 = (bf16[2,256,128]{2,1,0:T(8,128)(2,1)S(1)}, bf16[2,256,128]{2,1,0:T(8,128)(2,1)S(1)}, u32[]{:S(2)}, u32[]{:S(2)}) collective-permute-start(bf16[2,256,128]{2,1,0:T(8,128)(2,1)S(1)} %get-tuple-element.23), channel_id=1, source_target_pairs={{0,4},{2,6},{4,0},{6,2},{8,12},{10,14},{12,8},{14,10},{1,5},{3,7},... | collective-permute-start | bytes 393224 | tf_op jit(solution)/shard_map/ppermute | solution.py:336
  39.2 0.5 collective-permute-start.11
  39.7 1.7 %collective-permute-done.6.refs_3_ = bf16[2,256,128]{2,1,0:T(8,128)(2,1)S(1)} collective-permute-done((bf16[2,256,128]{2,1,0:T(8,128)(2,1)S(1)}, bf16[2,256,128]{2,1,0:T(8,128)(2,1)S(1)}, u32[]{:S(2)}, u32[]{:S(2)}) %collective-permute-start.6) | collective-permute-done | bytes 131104 | tf_op jit(solution)/shard_map/ppermute | solution.py:336
  41.4 0.5 collective-permute-start.13
  41.9 2.6 %collective-permute-done.5.refs_2_ = bf16[2,256,128]{2,1,0:T(8,128)(2,1)S(1)} collective-permute-done((bf16[2,256,128]{2,1,0:T(8,128)(2,1)S(1)}, bf16[2,256,128]{2,1,0:T(8,128)(2,1)S(1)}, u32[]{:S(2)}, u32[]{:S(2)}) %collective-permute-start.5) | collective-permute-done | bytes 131104 | tf_op jit(solution)/shard_map/ppermute | solution.py:336
  44.5 0.5 collective-permute-start.10
  45.2 0.4 collective-permute-start.9
  45.6 0.3 collective-permute-done.14.refs_15_
  46.1 0.3 collective-permute-done.8.refs_9_
  46.7 0.7 copy-done.25
  47.4 5.6 %all-to-all-done.1 = bf16[32,64,128]{2,1,0:T(8,128)(2,1)S(1)} async-done(((bf16[32,64,128]{2,1,0:T(8,128)(2,1)}), bf16[32,64,128]{2,1,0:T(8,128)(2,1)S(1)}, u32[]{:S(2)}, u32[]{:S(2)}) %all-to-all-start.1) | async-done | bytes 524320 | tf_op jit(solution)/shard_map/all_to_all | solution.py:347
  52.9 0.8 copy-done.15
  53.8 6.6 %far.1 = bf16[32,80,128]{2,1,0:T(8,128)(2,1)} custom-call(bf16[2048,128]{1,0:T(8,128)(2,1)} %bitcast.3, bf16[2,256,128]{2,1,0:T(8,128)(2,1)} %copy-done.10, bf16[2,256,128]{2,1,0:T(8,128)(2,1)} %copy-done.17, bf16[2,256,128]{2,1,0:T(8,128)(2,1)} %copy-done.18, bf16[2,256,128]{2,1,0:T(8,128)(2,1)} %copy-done.16, bf16[2,256,128]{2,1,0:T(8,128)(2,1)} %copy-done.2, ...), custom_call_target="tpu_custom_call" | custom-call | tf_op jit(solution)/shard_map/far/pallas_call | solution.py:375
  60.5 10.2 %all-to-all-start.2 = ((bf16[32,80,128]{2,1,0:T(8,128)(2,1)}), bf16[32,80,128]{2,1,0:T(8,128)(2,1)S(1)}, u32[]{:S(2)}, u32[]{:S(2)}) async-start(bf16[32,80,128]{2,1,0:T(8,128)(2,1)} %far.1), calls=%async_computation.2 | async-start | bytes 1310720 | tf_op jit(solution)/shard_map/all_to_all | solution.py:391
  70.8 1.6 %copy-done.1 = bf16[8,256,512]{2,1,0:T(8,128)(2,1)S(1)} copy-done((bf16[8,256,512]{2,1,0:T(8,128)(2,1)S(1)}, bf16[8,256,512]{2,1,0:T(8,128)(2,1)}, u32[]{:S(2)}) %copy-start.1) | copy-done | bytes 2097176
  72.3 4.0 %near.1 = (f32[32,8,128]{2,1,0:T(8,128)S(1)}, f32[32,8,128]{2,1,0:T(8,128)S(1)}) custom-call(s32[8]{0:T(128)S(1)} %copy-done.14, bf16[8,4096]{1,0:T(8,128)(2,1)S(1)} %copy-done.9, bf16[8,512]{1,0:T(8,128)(2,1)S(1)} %copy-done.11, bf16[8,512]{1,0:T(8,128)(2,1)S(1)} %copy-done.12, bf16[8,256,512]{2,1,0:T(8,128)(2,1)S(1)} %copy-done, ...), custom_call_target="tpu_custom_call" | custom-call | flops 300000000 | bytes 4500000 | tf_op jit(solution)/shard_map/near/pallas_call | solution.py:349
  76.3 13.7 %all-to-all-done.2.back_ref = bf16[32,80,128]{2,1,0:T(8,128)(2,1)S(1)} async-done(((bf16[32,80,128]{2,1,0:T(8,128)(2,1)}), bf16[32,80,128]{2,1,0:T(8,128)(2,1)S(1)}, u32[]{:S(2)}, u32[]{:S(2)}) %all-to-all-start.2) | async-done | bytes 655392 | tf_op jit(solution)/shard_map/all_to_all | solution.py:391
  90.0 0.5 select.1
  90.5 8.1 %all_to_all.21.back_ref = bf16[4,80,128]{2,1,0:T(8,128)(2,1)S(1)} all-to-all(bf16[4,80,128]{2,1,0:T(8,128)(2,1)S(1)} %select.1), channel_id=1, replica_groups=mesh['xh'=2,'z'=8,'xl'=2,'y'=4,'c'=2] {'y'}, dimensions={0} | all-to-all | bytes 163840 | tf_op jit(solution)/shard_map/all_to_all | solution.py:400
  98.6 0.8 merge.1
  (62 shorter events, 0.9 us)
Async XLA Ops:
  4.4 49.4 %copy-start.10 = (bf16[2,256,128]{2,1,0:T(8,128)(2,1)}, bf16[2,256,128]{2,1,0:T(8,128)(2,1)S(1)}, u32[]{:S(2)}) copy-start(bf16[2,256,128]{2,1,0:T(8,128)(2,1)S(1)} %get-tuple-element.21.refs_0_) | copy-start | bytes 393220
  4.4 17.3 %collective-permute-start = (bf16[2,256,128]{2,1,0:T(8,128)(2,1)S(1)}, bf16[2,256,128]{2,1,0:T(8,128)(2,1)S(1)}, u32[]{:S(2)}, u32[]{:S(2)}) collective-permute-start(bf16[2,256,128]{2,1,0:T(8,128)(2,1)S(1)} %get-tuple-element.17), channel_id=1, source_target_pairs={{0,8},{2,10},{4,12},{6,14},{8,0},{10,2},{12,4},{14,6},{1,9},{3,11}... | collective-permute-start | bytes 393224 | tf_op jit(solution)/shard_map/ppermute | solution.py:336
  5.9 15.7 %collective-permute-start.1 = (bf16[2,256,128]{2,1,0:T(8,128)(2,1)S(1)}, bf16[2,256,128]{2,1,0:T(8,128)(2,1)S(1)}, u32[]{:S(2)}, u32[]{:S(2)}) collective-permute-start(bf16[2,256,128]{2,1,0:T(8,128)(2,1)S(1)} %get-tuple-element.18), channel_id=1, source_target_pairs={{0,10},{2,8},{4,14},{6,12},{8,2},{10,0},{12,6},{14,4},{1,11},{3,9}... | collective-permute-start | bytes 393224 | tf_op jit(solution)/shard_map/ppermute | solution.py:336
  7.5 14.2 %collective-permute-start.2 = (bf16[2,256,128]{2,1,0:T(8,128)(2,1)S(1)}, bf16[2,256,128]{2,1,0:T(8,128)(2,1)S(1)}, u32[]{:S(2)}, u32[]{:S(2)}) collective-permute-start(bf16[2,256,128]{2,1,0:T(8,128)(2,1)S(1)} %get-tuple-element.19), channel_id=1, source_target_pairs={{0,12},{2,14},{4,8},{6,10},{8,4},{10,6},{12,0},{14,2},{1,13},{3,15... | collective-permute-start | bytes 393224 | tf_op jit(solution)/shard_map/ppermute | solution.py:336
  11.3 10.3 %collective-permute-start.3 = (bf16[2,256,128]{2,1,0:T(8,128)(2,1)S(1)}, bf16[2,256,128]{2,1,0:T(8,128)(2,1)S(1)}, u32[]{:S(2)}, u32[]{:S(2)}) collective-permute-start(bf16[2,256,128]{2,1,0:T(8,128)(2,1)S(1)} %get-tuple-element.20), channel_id=1, source_target_pairs={{0,14},{2,12},{4,10},{6,8},{8,6},{10,4},{12,2},{14,0},{1,15},{3,13... | collective-permute-start | bytes 393224 | tf_op jit(solution)/shard_map/ppermute | solution.py:336
  21.6 32.1 %copy-start.2 = (bf16[2,256,128]{2,1,0:T(8,128)(2,1)}, bf16[2,256,128]{2,1,0:T(8,128)(2,1)S(1)}, u32[]{:S(2)}) copy-start(bf16[2,256,128]{2,1,0:T(8,128)(2,1)S(1)} %collective-permute-done.refs_0_.refs_4_) | copy-start | bytes 393220
  21.6 32.1 %copy-start.3 = (bf16[2,256,128]{2,1,0:T(8,128)(2,1)}, bf16[2,256,128]{2,1,0:T(8,128)(2,1)S(1)}, u32[]{:S(2)}) copy-start(bf16[2,256,128]{2,1,0:T(8,128)(2,1)S(1)} %collective-permute-done.1.refs_1_.refs_5_) | copy-start | bytes 393220
  21.7 32.1 %copy-start.4 = (bf16[2,256,128]{2,1,0:T(8,128)(2,1)}, bf16[2,256,128]{2,1,0:T(8,128)(2,1)S(1)}, u32[]{:S(2)}) copy-start(bf16[2,256,128]{2,1,0:T(8,128)(2,1)S(1)} %collective-permute-done.2.refs_2_.refs_6_) | copy-start | bytes 393220
  21.7 32.1 %copy-start.5 = (bf16[2,256,128]{2,1,0:T(8,128)(2,1)}, bf16[2,256,128]{2,1,0:T(8,128)(2,1)S(1)}, u32[]{:S(2)}) copy-start(bf16[2,256,128]{2,1,0:T(8,128)(2,1)S(1)} %collective-permute-done.3.refs_3_.refs_7_) | copy-start | bytes 393220
  23.2 29.8 %all-to-all-start.1 = ((bf16[32,64,128]{2,1,0:T(8,128)(2,1)}), bf16[32,64,128]{2,1,0:T(8,128)(2,1)S(1)}, u32[]{:S(2)}, u32[]{:S(2)}) async-start(bf16[32,64,128]{2,1,0:T(8,128)(2,1)} %bitcast.1), calls=%async_computation.1 | async-start | bytes 1048576 | tf_op jit(solution)/shard_map/all_to_all | solution.py:347
  34.4 7.0 %collective-permute-start.6 = (bf16[2,256,128]{2,1,0:T(8,128)(2,1)S(1)}, bf16[2,256,128]{2,1,0:T(8,128)(2,1)S(1)}, u32[]{:S(2)}, u32[]{:S(2)}) collective-permute-start(bf16[2,256,128]{2,1,0:T(8,128)(2,1)S(1)} %get-tuple-element.24), channel_id=1, source_target_pairs={{0,6},{2,4},{4,2},{6,0},{8,14},{10,12},{12,10},{14,8},{1,7},{3,5},... | collective-permute-start | bytes 393224 | tf_op jit(solution)/shard_map/ppermute | solution.py:336
  35.4 6.1 %collective-permute-start.4 = (bf16[2,256,128]{2,1,0:T(8,128)(2,1)S(1)}, bf16[2,256,128]{2,1,0:T(8,128)(2,1)S(1)}, u32[]{:S(2)}, u32[]{:S(2)}) collective-permute-start(bf16[2,256,128]{2,1,0:T(8,128)(2,1)S(1)} %get-tuple-element.22), channel_id=1, source_target_pairs={{0,2},{2,0},{4,6},{6,4},{8,10},{10,8},{12,14},{14,12},{1,3},{3,1},... | collective-permute-start | bytes 393224 | tf_op jit(solution)/shard_map/ppermute | solution.py:336
  35.4 9.2 %collective-permute-start.5 = (bf16[2,256,128]{2,1,0:T(8,128)(2,1)S(1)}, bf16[2,256,128]{2,1,0:T(8,128)(2,1)S(1)}, u32[]{:S(2)}, u32[]{:S(2)}) collective-permute-start(bf16[2,256,128]{2,1,0:T(8,128)(2,1)S(1)} %get-tuple-element.23), channel_id=1, source_target_pairs={{0,4},{2,6},{4,0},{6,2},{8,12},{10,14},{12,8},{14,10},{1,5},{3,7},... | collective-permute-start | bytes 393224 | tf_op jit(solution)/shard_map/ppermute | solution.py:336
  39.2 5.4 %collective-permute-start.7 = (bf16[2,256,128]{2,1,0:T(8,128)(2,1)S(1)}, bf16[2,256,128]{2,1,0:T(8,128)(2,1)S(1)}, u32[]{:S(2)}, u32[]{:S(2)}) collective-permute-start(bf16[2,256,128]{2,1,0:T(8,128)(2,1)S(1)} %get-tuple-element.21.refs_0_), channel_id=1, source_target_pairs={{0,1},{1,0},{2,3},{3,2},{4,5},{5,4},{6,7},{7,6},{8,9},{9,8},{10,11... | collective-permute-start | bytes 393224 | tf_op jit(solution)/shard_map/ppermute | solution.py:337
  39.2 5.9 %collective-permute-start.11 = (bf16[2,256,128]{2,1,0:T(8,128)(2,1)S(1)}, bf16[2,256,128]{2,1,0:T(8,128)(2,1)S(1)}, u32[]{:S(2)}, u32[]{:S(2)}) collective-permute-start(bf16[2,256,128]{2,1,0:T(8,128)(2,1)S(1)} %collective-permute-done.refs_0_.refs_4_), channel_id=1, source_target_pairs={{0,1},{1,0},{2,3},{3,2},{4,5},{5,4},{6,7},{7,6},{8,9},{9,8},{10,11... | collective-permute-start | bytes 393224 | tf_op jit(solution)/shard_map/ppermute | solution.py:337
  41.4 5.0 %copy-start.16 = (bf16[2,256,128]{2,1,0:T(8,128)(2,1)}, bf16[2,256,128]{2,1,0:T(8,128)(2,1)S(1)}, u32[]{:S(2)}) copy-start(bf16[2,256,128]{2,1,0:T(8,128)(2,1)S(1)} %collective-permute-done.6.refs_3_) | copy-start | bytes 393220
  41.4 3.7 %collective-permute-start.12 = (bf16[2,256,128]{2,1,0:T(8,128)(2,1)S(1)}, bf16[2,256,128]{2,1,0:T(8,128)(2,1)S(1)}, u32[]{:S(2)}, u32[]{:S(2)}) collective-permute-start(bf16[2,256,128]{2,1,0:T(8,128)(2,1)S(1)} %collective-permute-done.1.refs_1_.refs_5_), channel_id=1, source_target_pairs={{0,1},{1,0},{2,3},{3,2},{4,5},{5,4},{6,7},{7,6},{8,9},{9,8},{10,11... | collective-permute-start | bytes 393224 | tf_op jit(solution)/shard_map/ppermute | solution.py:337
  41.4 5.0 %copy-start.17 = (bf16[2,256,128]{2,1,0:T(8,128)(2,1)}, bf16[2,256,128]{2,1,0:T(8,128)(2,1)S(1)}, u32[]{:S(2)}) copy-start(bf16[2,256,128]{2,1,0:T(8,128)(2,1)S(1)} %collective-permute-done.4.refs_1_) | copy-start | bytes 393220
  41.4 4.1 %collective-permute-start.13 = (bf16[2,256,128]{2,1,0:T(8,128)(2,1)S(1)}, bf16[2,256,128]{2,1,0:T(8,128)(2,1)S(1)}, u32[]{:S(2)}, u32[]{:S(2)}) collective-permute-start(bf16[2,256,128]{2,1,0:T(8,128)(2,1)S(1)} %collective-permute-done.2.refs_2_.refs_6_), channel_id=1, source_target_pairs={{0,1},{1,0},{2,3},{3,2},{4,5},{5,4},{6,7},{7,6},{8,9},{9,8},{10,11... | collective-permute-start | bytes 393224 | tf_op jit(solution)/shard_map/ppermute | solution.py:337
  44.5 1.3 %collective-permute-start.14 = (bf16[2,256,128]{2,1,0:T(8,128)(2,1)S(1)}, bf16[2,256,128]{2,1,0:T(8,128)(2,1)S(1)}, u32[]{:S(2)}, u32[]{:S(2)}) collective-permute-start(bf16[2,256,128]{2,1,0:T(8,128)(2,1)S(1)} %collective-permute-done.3.refs_3_.refs_7_), channel_id=1, source_target_pairs={{0,1},{1,0},{2,3},{3,2},{4,5},{5,4},{6,7},{7,6},{8,9},{9,8},{10,11... | collective-permute-start | bytes 393224 | tf_op jit(solution)/shard_map/ppermute | solution.py:337
  44.5 1.5 %collective-permute-start.10 = (bf16[2,256,128]{2,1,0:T(8,128)(2,1)S(1)}, bf16[2,256,128]{2,1,0:T(8,128)(2,1)S(1)}, u32[]{:S(2)}, u32[]{:S(2)}) collective-permute-start(bf16[2,256,128]{2,1,0:T(8,128)(2,1)S(1)} %collective-permute-done.6.refs_3_), channel_id=1, source_target_pairs={{0,1},{1,0},{2,3},{3,2},{4,5},{5,4},{6,7},{7,6},{8,9},{9,8},{10,11... | collective-permute-start | bytes 393224 | tf_op jit(solution)/shard_map/ppermute | solution.py:337
  45.0 1.3 %collective-permute-start.8 = (bf16[2,256,128]{2,1,0:T(8,128)(2,1)S(1)}, bf16[2,256,128]{2,1,0:T(8,128)(2,1)S(1)}, u32[]{:S(2)}, u32[]{:S(2)}) collective-permute-start(bf16[2,256,128]{2,1,0:T(8,128)(2,1)S(1)} %collective-permute-done.4.refs_1_), channel_id=1, source_target_pairs={{0,1},{1,0},{2,3},{3,2},{4,5},{5,4},{6,7},{7,6},{8,9},{9,8},{10,11... | collective-permute-start | bytes 393224 | tf_op jit(solution)/shard_map/ppermute | solution.py:337
  45.2 8.6 %copy-start.21 = (bf16[2,256,128]{2,1,0:T(8,128)(2,1)}, bf16[2,256,128]{2,1,0:T(8,128)(2,1)S(1)}, u32[]{:S(2)}) copy-start(bf16[2,256,128]{2,1,0:T(8,128)(2,1)S(1)} %collective-permute-done.12.refs_13_) | copy-start | bytes 393220
  45.2 2.2 %collective-permute-start.9 = (bf16[2,256,128]{2,1,0:T(8,128)(2,1)S(1)}, bf16[2,256,128]{2,1,0:T(8,128)(2,1)}, u32[]{:S(2)}, u32[]{:S(2)}) collective-permute-start(bf16[2,256,128]{2,1,0:T(8,128)(2,1)S(1)} %collective-permute-done.5.refs_2_), channel_id=1, source_target_pairs={{0,1},{1,0},{2,3},{3,2},{4,5},{5,4},{6,7},{7,6},{8,9},{9,8},{10,11... | collective-permute-start | bytes 393224 | tf_op jit(solution)/shard_map/ppermute | solution.py:337
  45.6 8.2 %copy-start.22 = (bf16[2,256,128]{2,1,0:T(8,128)(2,1)}, bf16[2,256,128]{2,1,0:T(8,128)(2,1)S(1)}, u32[]{:S(2)}) copy-start(bf16[2,256,128]{2,1,0:T(8,128)(2,1)S(1)} %collective-permute-done.13.refs_14_) | copy-start | bytes 393220
  45.9 7.9 %copy-start.23 = (bf16[2,256,128]{2,1,0:T(8,128)(2,1)}, bf16[2,256,128]{2,1,0:T(8,128)(2,1)S(1)}, u32[]{:S(2)}) copy-start(bf16[2,256,128]{2,1,0:T(8,128)(2,1)S(1)} %collective-permute-done.14.refs_15_) | copy-start | bytes 393220
  53.8 16.9 %copy-start = (bf16[8,256,512]{2,1,0:T(8,128)(2,1)S(1)}, bf16[8,256,512]{2,1,0:T(8,128)(2,1)}, u32[]{:S(2)}) copy-start(bf16[8,256,512]{2,1,0:T(8,128)(2,1)} %key_ref.3) | copy-start | bytes 6291460
  53.8 16.9 %copy-start.9 = (bf16[8,4096]{1,0:T(8,128)(2,1)S(1)}, bf16[8,4096]{1,0:T(8,128)(2,1)}, u32[]{:S(2)}) copy-start(bf16[8,4096]{1,0:T(8,128)(2,1)} %query_ref.1) | copy-start | bytes 196612
  53.8 16.9 %copy-start.11 = (bf16[8,512]{1,0:T(8,128)(2,1)S(1)}, bf16[8,512]{1,0:T(8,128)(2,1)}, u32[]{:S(2)}) copy-start(bf16[8,512]{1,0:T(8,128)(2,1)} %new_key_ref.1) | copy-start | bytes 24580
  53.8 16.9 %copy-start.12 = (bf16[8,512]{1,0:T(8,128)(2,1)S(1)}, bf16[8,512]{1,0:T(8,128)(2,1)}, u32[]{:S(2)}) copy-start(bf16[8,512]{1,0:T(8,128)(2,1)} %new_value_ref.1) | copy-start | bytes 24580
  53.8 16.9 %copy-start.14 = (s32[8]{0:T(128)S(1)}, s32[8]{0:T(128)}, u32[]{:S(2)}) copy-start(s32[8]{0:T(128)} %len_ref.1) | copy-start | bytes 100
  60.5 29.6 %all-to-all-start.2 = ((bf16[32,80,128]{2,1,0:T(8,128)(2,1)}), bf16[32,80,128]{2,1,0:T(8,128)(2,1)S(1)}, u32[]{:S(2)}, u32[]{:S(2)}) async-start(bf16[32,80,128]{2,1,0:T(8,128)(2,1)} %far.1), calls=%async_computation.2 | async-start | bytes 1310720 | tf_op jit(solution)/shard_map/all_to_all | solution.py:391
  (11 other events, 12.4 us)
where the time goes:
time: 101 us; the launch traced here: 99.4 us
  starting transfers between devices  35.4 us (35%)
  waiting for transfers between devices  24.4 us (24%)
  blocking collectives  18.2 us (18%)
  Pallas kernels  14.1 us (14%)
  local copies, waits for them, and re-layouts  6.99 us (7%)
    all_to_all x1, waiting for transfers between devices, shards(): back = lax.all_to_all(parcel, FAR, 0, 0, tiled=True)  13.7 us
    ppermute x7, starting transfers between devices, shards(): lax.ppermute(cuts[step], NEAR, [(i, i ^ step) for i in range(8)])  11.9 us
    all_to_all x1, starting transfers between devices, shards(): lax.all_to_all(outgoing.reshape(PROMPTS, 64, HD), FAR, 0, 0, tiled=True)  11.2 us
    all_to_all x1, starting transfers between devices, shards(): back = lax.all_to_all(parcel, FAR, 0, 0, tiled=True)  10.2 us
    all_to_all x1, blocking collectives, shards(): got = lax.all_to_all(sent, 'y', 0, 0, tiled=True)  10.1 us
    all_to_all x1, blocking collectives, shards(): final = lax.all_to_all(chosen, 'y', 0, 0, tiled=True)  8.08 us
    unnamed x52, local copies, waits for them, and re-layouts  6.99 us
    pallas_call x1, Pallas kernels, shards(): pl.pallas_call(far_kernel, out_shape=jax.ShapeDtypeStruct((PROMPTS, 80, H...  6.61 us
  transfers between devices with their start and end apart: 17, of which 7 were waited for; matrix products, arithmetic and copies ran while one was open for 0% of the time, Pallas kernels for 4%

commit v1 on v0

--- a/solution.py
+++ b/solution.py
@@ -44,7 +44,7 @@
     return picked
 
 
-def prep_kernel(place_ref, prompt_hbm, query_hbm, key_ref, value_ref, send_ref, *refs):
+def prep_kernel(place_ref, prompt_hbm, query_hbm, key_ref, value_ref, out_ref, tag_ref, *refs):
     cut_refs = refs[:8]
     prompt_ref, query_ref, small_sem, cut_sem = refs[8:]
     small = [
@@ -69,39 +69,23 @@
     for copy in small:
         copy.wait()
     slots = slots_of(prompt_ref)
-    lane = lax.broadcasted_iota(jnp.int32, (HELD, HD), 1)
-    row = lax.broadcasted_iota(jnp.int32, (HELD, HD), 0)
-    tags = jnp.concatenate(
-        [spread(slots, lane & 7).astype(jnp.float32), spread(slots, row).astype(jnp.float32)], axis=0
+    row = lax.broadcasted_iota(jnp.int32, (16, HD), 0)
+    tag_ref[...] = spread(slots, row & 7).astype(jnp.float32).astype(jnp.bfloat16)
+    held = jnp.concatenate(
+        [query_ref[:, h * HD : (h + 1) * HD].astype(jnp.float32) for h in range(HEADS)], axis=0
     ).astype(jnp.bfloat16)
-    for y in range(KVH):
-        send_ref[y, :64] = jnp.concatenate(
-            [
-                query_ref[:, h * HD : (h + 1) * HD].astype(jnp.float32)
-                for h in range(y * RATIO, (y + 1) * RATIO)
-            ],
-            axis=0,
-        ).astype(jnp.bfloat16)
-        send_ref[y, 64:] = tags
-    for copy in copies:
-        copy.wait()
-
-
-def pack_kernel(got_ref, *refs):
-    out_ref = refs[-1]
-    held = got_ref[:, :64].reshape(256, HD)
-    tags = [got_ref[y, 64:].astype(jnp.float32)[:1].astype(jnp.int32) for y in range(KVH)]
-    half = lax.broadcasted_iota(jnp.int32, (1, HD), 1) < 64
-    tag = jnp.concatenate([jnp.where(half, tags[0], tags[1]), jnp.where(half, tags[2], tags[3])], axis=1)
-    lane_key = (lax.broadcasted_iota(jnp.int32, (1, 256), 1) >> 3) * 64 + tag
+    lane = lax.broadcasted_iota(jnp.int32, (1, HEADS * HELD), 1)
+    lane_key = (lane >> 3) * 64 + spread(slots, lane & 7)
     chunk = 512
     for start in range(0, ROWS, chunk):
         row = lax.broadcasted_iota(jnp.int32, (chunk, 1), 0) + start
-        row_key = ((row >> 1) & 3) * 512 + ((row >> 3) & 7) * 64 + (row >> 6) * 2 + (row & 1)
+        row_key = (((row >> 4) & 3) * 8 + (row & 7)) * 64 + (row >> 6) * 2 + ((row >> 3) & 1)
         select = (row_key == lane_key).astype(jnp.float32).astype(jnp.bfloat16)
         out_ref[start : start + chunk, :] = jnp.dot(
             select, held, preferred_element_type=jnp.float32
         ).astype(jnp.bfloat16)
+    for copy in copies:
+        copy.wait()
 
 
 def near_kernel(
@@ -170,7 +154,7 @@
 
 def far_kernel(query_ref, *refs):
     sources = refs[:16]
-    out_ref, score_ref, query_scr, mixed_scr, stat_scr, cache_ref, sems = refs[16:]
+    out_ref, score_ref, wide_scr, query_scr, mixed_scr, stat_scr, cache_ref, sems = refs[16:]
     copies = [
         pltpu.make_async_copy(source, cache_ref.at[n], sems.at[n]) for n, source in enumerate(sources)
     ]
@@ -180,8 +164,12 @@
     span = 32
     block = span * RATIO
     tokens = 16 * PIECE
-    queries = query_ref[...].astype(jnp.float32).reshape(32, RATIO, 8, HD)
-    biggest = jnp.max(jnp.max(jnp.abs(queries), axis=1).reshape(SLOTS, HD), axis=1, keepdims=True)
+    wide_scr[...] = query_ref[...].astype(jnp.float32)
+    queries = [wide_scr[pl.ds(h, SLOTS, RATIO), :] for h in range(RATIO)]
+    biggest = jnp.abs(queries[0])
+    for h in range(1, RATIO):
+        biggest = jnp.maximum(biggest, jnp.abs(queries[h]))
+    biggest = jnp.max(biggest, axis=1, keepdims=True)
     valid = (biggest > 0).astype(jnp.float32)
     row = lax.broadcasted_iota(jnp.int32, (SLOTS, SLOTS), 0)
     lane = lax.broadcasted_iota(jnp.int32, (SLOTS, SLOTS), 1)
@@ -195,7 +183,7 @@
     for h in range(RATIO):
         query_scr[h] = lax.dot_general(
             gather,
-            queries[:, h].reshape(SLOTS, HD).astype(jnp.bfloat16),
+            queries[h].astype(jnp.bfloat16),
             (((0,), (0,)), ((), ())),
             preferred_element_type=jnp.float32,
         ).astype(jnp.bfloat16)
@@ -257,23 +245,31 @@
     return stat
 
 
-def select_kernel(got_ref, back_ref, *refs):
+def select_kernel(place_ref, back_ref, *refs):
+    tag_refs = refs[:4]
     send_ref = refs[-1]
-    tags = [got_ref[y, 64:].astype(jnp.float32)[8:, :1].astype(jnp.int32) for y in range(KVH)]
+    sources = [(place_ref[0] & 3) ^ step for step in range(4)]
+    tags = [tag_ref[...].astype(jnp.float32)[:8, :1].astype(jnp.int32) for tag_ref in tag_refs]
     lane = lax.broadcasted_iota(jnp.int32, (1, ROWS), 1)
     lane_key = ((lane >> 1) & 3) * 512 + ((lane >> 3) & 7) * 64 + (lane >> 6) * 2 + (lane & 1)
-    tag = jnp.concatenate([tags[y] for y in range(KVH) for _ in range(RATIO)], axis=0)
-    row_key = (lax.broadcasted_iota(jnp.int32, (256, 1), 0) >> 3) * 64 + tag
+    row_key = jnp.concatenate(
+        [tags[s] + (sources[s] * 512 + h * 64) for s in range(4) for h in range(RATIO)], axis=0
+    )
     select = (row_key == lane_key).astype(jnp.float32).astype(jnp.bfloat16)
     far = jnp.dot(select, back_ref[:, :64].reshape(ROWS, HD), preferred_element_type=jnp.float32)
-    send_ref[:, :64] = far.astype(jnp.bfloat16).reshape(KVH, 64, HD)
+    for s in range(4):
+        send_ref[sources[s], :64] = far[s * 64 : (s + 1) * 64].astype(jnp.bfloat16)
     stats = back_ref[:, 64:].astype(jnp.float32)[:, :8].reshape(SLOTS, HD).astype(jnp.bfloat16)
     lane = lax.broadcasted_iota(jnp.int32, (1, SLOTS), 1)
     lane_key = ((lane >> 1) & 3) * 64 + (lane >> 3) * 2 + (lane & 1)
-    row_key = (lax.broadcasted_iota(jnp.int32, (32, 1), 0) >> 3) * 64 + jnp.concatenate(tags, axis=0)
+    row_key = jnp.concatenate([tags[s] + sources[s] * 64 for s in range(4)], axis=0)
     select = (row_key == lane_key).astype(jnp.float32).astype(jnp.bfloat16)
-    stat = jnp.dot(select, stats, preferred_element_type=jnp.float32).reshape(KVH, 8, HD)
-    send_ref[:, 64:] = jnp.concatenate([stat, jnp.zeros_like(stat)], axis=1).astype(jnp.bfloat16)
+    stat = jnp.dot(select, stats, preferred_element_type=jnp.float32)
+    for s in range(4):
+        mine = stat[s * 8 : (s + 1) * 8]
+        send_ref[sources[s], 64:] = jnp.concatenate([mine, jnp.zeros_like(mine)], axis=0).astype(
+            jnp.bfloat16
+        )
 
 
 def merge_kernel(back_ref, near_ref, near_lse_ref, out_ref):
@@ -297,7 +293,6 @@
 VMEM = pl.BlockSpec(memory_space=pltpu.VMEM)
 SMEM = pl.BlockSpec(memory_space=pltpu.SMEM)
 ANY = pl.BlockSpec(memory_space=pl.ANY)
-HBM = pl.BlockSpec(memory_space=pltpu.HBM)
 
 
 def params(mib):
@@ -316,35 +311,32 @@
     prefix_value,
 ):
     place = lax.axis_index(NEAR).astype(jnp.int32).reshape(1)
-    sent, *cuts = pl.pallas_call(
+    outgoing, tag, *cuts = pl.pallas_call(
         prep_kernel,
-        out_shape=[jax.ShapeDtypeStruct((KVH, 80, HD), jnp.bfloat16)]
+        out_shape=[
+            jax.ShapeDtypeStruct((ROWS, HD), jnp.bfloat16),
+            jax.ShapeDtypeStruct((16, HD), jnp.bfloat16),
+        ]
         + [jax.ShapeDtypeStruct((2, PIECE, HD), jnp.bfloat16)] * 8,
-        in_specs=[SMEM, HBM, HBM, HBM, HBM],
-        out_specs=[VMEM] * 9,
+        in_specs=[SMEM, ANY, ANY, ANY, ANY],
+        out_specs=[VMEM] * 2 + [ANY] * 8,
         scratch_shapes=[
             pltpu.SMEM((HELD,), jnp.int32),
             pltpu.VMEM((HELD, HEADS * HD), jnp.bfloat16),
             pltpu.SemaphoreType.DMA((2,)),
             pltpu.SemaphoreType.DMA((8, 2)),
         ],
-        compiler_params=params(12),
+        compiler_params=params(60),
         name="prep",
     )(place, prompt_of, query, prefix_key, prefix_value)
+    arrived = lax.all_to_all(outgoing.reshape(128, 16, HD), FAR + ("y",), 0, 0, tiled=True)
     held = [cuts[0]]
     for step in range(1, 8):
         held.append(lax.ppermute(cuts[step], NEAR, [(i, i ^ step) for i in range(8)]))
     swapped = [lax.ppermute(piece, "c", [(0, 1), (1, 0)]) for piece in held]
-    got = lax.all_to_all(sent, "y", 0, 0, tiled=True)
-    outgoing = pl.pallas_call(
-        pack_kernel,
-        out_shape=jax.ShapeDtypeStruct((ROWS, HD), jnp.bfloat16),
-        in_specs=[VMEM] + [ANY] * 4,
-        out_specs=VMEM,
-        compiler_params=params(8),
-        name="pack",
-    )(got, *held[4:])
-    arrived = lax.all_to_all(outgoing.reshape(PROMPTS, 64, HD), FAR, 0, 0, tiled=True)
+    tags = [tag]
+    for step in range(1, 4):
+        tags.append(lax.ppermute(tag, "y", [(i, i ^ step) for i in range(4)]))
 
     near_out, near_lse = pl.pallas_call(
         near_kernel,
@@ -379,6 +371,7 @@
         out_specs=VMEM,
         scratch_shapes=[
             pltpu.VMEM((16, 256, PIECE), jnp.float32),
+            pltpu.VMEM((ROWS, HD), jnp.float32),
             pltpu.VMEM((RATIO, SLOTS, HD), jnp.bfloat16),
             pltpu.VMEM((RATIO, SLOTS, HD), jnp.bfloat16),
             pltpu.VMEM((SLOTS, HD), jnp.bfloat16),
@@ -392,11 +385,11 @@
     chosen = pl.pallas_call(
         select_kernel,
         out_shape=jax.ShapeDtypeStruct((KVH, 80, HD), jnp.bfloat16),
-        in_specs=[VMEM] * 2 + [ANY] * 2,
+        in_specs=[SMEM] + [VMEM] * 5 + [ANY] * 2,
         out_specs=VMEM,
         compiler_params=params(8),
         name="select",
-    )(got, back, near_out, near_lse)
+    )(place, back, *tags, near_out, near_lse)
     final = lax.all_to_all(chosen, "y", 0, 0, tiled=True)
     return pl.pallas_call(
         merge_kernel,

time: 101 us -> 127 us (1.26); the launches traced: 99.4 us -> 127 us
  Pallas kernels: 14.1 us -> 45.9 us
  blocking collectives: 18.2 us -> 8.08 us
  starting transfers between devices: 35.4 us -> 44.6 us
  local copies, waits for them, and re-layouts: 6.99 us -> 2.99 us
    pallas_call x2 -> x1, Pallas kernels: 2.25 us -> 33.8 us  [shards(): pl.pallas_call(prep_kernel, out_shape=[jax.ShapeDtypeStruct((ROWS, HD), j...]
    all_to_all x1 -> x0, blocking collectives: 10.1 us -> none  [shards(): got = lax.all_to_all(sent, 'y', 0, 0, tiled=True)]
    ppermute x7, waiting for transfers between devices: 4.34 us -> 12.6 us  [shards(): lax.ppermute(cuts[step], NEAR, [(i, i ^ step) for i in range(8)])]
    all_to_all x1, waiting for transfers between devices: 5.56 us -> 0.01 us  [shards(): lax.all_to_all(outgoing.reshape(128, 16, HD), FAR + ('y',), 0, 0, tiled=T...]
    ppermute x0 -> x3, starting transfers between devices: none -> 4.79 us  [shards(): tags.append(lax.ppermute(tag, 'y', [(i, i ^ step) for i in range(4)]))]
    unnamed x52 -> x46, local copies, waits for them, and re-layouts: 6.99 us -> 2.99 us
    all_to_all x1, starting transfers between devices: 11.2 us -> 15 us  [shards(): lax.all_to_all(outgoing.reshape(128, 16, HD), FAR + ('y',), 0, 0, tiled=T...]
    all_to_all x1, waiting for transfers between devices: 13.7 us -> 11.1 us  [shards(): back = lax.all_to_all(parcel, FAR, 0, 0, tiled=True)]
  transfers between devices with their start and end apart: 17 -> 20, of which waited for: 7 -> 10; matrix products, arithmetic and copies ran while one was open for 0% -> 0% of each run, Pallas kernels for 4% -> 3%
where the time goes in v1:
time: 127 us
  Pallas kernels  45.9 us (36%)
  starting transfers between devices  44.6 us (35%)
  waiting for transfers between devices  24.9 us (20%)
  blocking collectives  8.08 us (6%)
  local copies, waits for them, and re-layouts  2.99 us (2%)
    pallas_call x1, Pallas kernels, shards(): pl.pallas_call(prep_kernel, out_shape=[jax.ShapeDtypeStruct((ROWS, HD), j...  33.8 us
    all_to_all x1, starting transfers between devices, shards(): lax.all_to_all(outgoing.reshape(128, 16, HD), FAR + ('y',), 0, 0, tiled=T...  15 us
    ppermute x7, waiting for transfers between devices, shards(): lax.ppermute(cuts[step], NEAR, [(i, i ^ step) for i in range(8)])  12.6 us
    all_to_all x1, starting transfers between devices, shards(): back = lax.all_to_all(parcel, FAR, 0, 0, tiled=True)  12.3 us
    all_to_all x1, waiting for transfers between devices, shards(): back = lax.all_to_all(parcel, FAR, 0, 0, tiled=True)  11.1 us
    ppermute x7, starting transfers between devices, shards(): lax.ppermute(cuts[step], NEAR, [(i, i ^ step) for i in range(8)])  11 us
    all_to_all x1, blocking collectives, shards(): final = lax.all_to_all(chosen, 'y', 0, 0, tiled=True)  8.08 us
    pallas_call x1, Pallas kernels, shards(): pl.pallas_call(far_kernel, out_shape=jax.ShapeDtypeStruct((PROMPTS, 80, H...  6.81 us
  transfers between devices with their start and end apart: 20, of which 10 were waited for; matrix products, arithmetic and copies ran while one was open for 0% of the time, Pallas kernels for 3%

profile of v1, /device:TPU:32, one launch (start us, length us, event | category | flops | bytes accessed | tf_op | source)
XLA Modules:
  0.0 126.7 jit_solution(763280591483171022)
XLA Ops:
  0.0 33.8 %prep.1 = (bf16[2048,128]{1,0:T(8,128)(2,1)}, bf16[16,128]{1,0:T(8,128)(2,1)}, bf16[2,256,128]{2,1,0:T(8,128)(2,1)}, bf16[2,256,128]{2,1,0:T(8,128)(2,1)}, bf16[...) custom-call(s32[1]{0:T(128)} %bitcast.place_ref, ...), custom_call_target="tpu_custom_call" | custom-call | tf_op jit(solution)/shard_map/prep/pallas_call | solution.py:314
  33.8 15.0 %all-to-all-start = ((bf16[128,16,128]{2,1,0:T(8,128)(2,1)}), bf16[128,16,128]{2,1,0:T(8,128)(2,1)S(1)}, u32[]{:S(2)}, u32[]{:S(2)}) async-start(bf16[128,16,128]{2,1,0:T(8,128)(2,1)} %bitcast.4), calls=%async_computation | async-start | bytes 1048576 | tf_op jit(solution)/shard_map/all_to_all | solution.py:332
  48.9 2.8 %collective-permute-start.2 = (bf16[2,256,128]{2,1,0:T(8,128)(2,1)}, bf16[2,256,128]{2,1,0:T(8,128)(2,1)S(1)}, u32[]{:S(2)}, u32[]{:S(2)}) collective-permute-start(bf16[2,256,128]{2,1,0:T(8,128)(2,1)} %get-tuple-element.21), channel_id=1, source_target_pairs={{0,6},{2,4},{4,2},{6,0},{8,14},{10,12},{12,10},{14,8},{1,7},{3,5},... | collective-permute-start | bytes 393224 | tf_op jit(solution)/shard_map/ppermute | solution.py:335
  51.6 1.5 %collective-permute-start.3 = (bf16[2,256,128]{2,1,0:T(8,128)(2,1)}, bf16[2,256,128]{2,1,0:T(8,128)(2,1)S(1)}, u32[]{:S(2)}, u32[]{:S(2)}) collective-permute-start(bf16[2,256,128]{2,1,0:T(8,128)(2,1)} %get-tuple-element.22), channel_id=1, source_target_pairs={{0,8},{2,10},{4,12},{6,14},{8,0},{10,2},{12,4},{14,6},{1,9},{3,11}... | collective-permute-start | bytes 393224 | tf_op jit(solution)/shard_map/ppermute | solution.py:335
  53.3 2.7 %collective-permute-start.5 = (bf16[2,256,128]{2,1,0:T(8,128)(2,1)}, bf16[2,256,128]{2,1,0:T(8,128)(2,1)S(1)}, u32[]{:S(2)}, u32[]{:S(2)}) collective-permute-start(bf16[2,256,128]{2,1,0:T(8,128)(2,1)} %get-tuple-element.24), channel_id=1, source_target_pairs={{0,12},{2,14},{4,8},{6,10},{8,4},{10,6},{12,0},{14,2},{1,13},{3,15... | collective-permute-start | bytes 393224 | tf_op jit(solution)/shard_map/ppermute | solution.py:335
  56.0 2.7 %collective-permute-start.6 = (bf16[2,256,128]{2,1,0:T(8,128)(2,1)}, bf16[2,256,128]{2,1,0:T(8,128)(2,1)S(1)}, u32[]{:S(2)}, u32[]{:S(2)}) collective-permute-start(bf16[2,256,128]{2,1,0:T(8,128)(2,1)} %get-tuple-element.25), channel_id=1, source_target_pairs={{0,14},{2,12},{4,10},{6,8},{8,6},{10,4},{12,2},{14,0},{1,15},{3,13... | collective-permute-start | bytes 393224 | tf_op jit(solution)/shard_map/ppermute | solution.py:335
  58.7 1.5 %collective-permute-done.3.refs_4_ = bf16[2,256,128]{2,1,0:T(8,128)(2,1)S(1)} collective-permute-done((bf16[2,256,128]{2,1,0:T(8,128)(2,1)}, bf16[2,256,128]{2,1,0:T(8,128)(2,1)S(1)}, u32[]{:S(2)}, u32[]{:S(2)}) %collective-permute-start.3) | collective-permute-done | bytes 131104 | tf_op jit(solution)/shard_map/ppermute | solution.py:335
  60.2 1.1 collective-permute-start.1
  61.4 2.8 %collective-permute-done.4.refs_5_ = bf16[2,256,128]{2,1,0:T(8,128)(2,1)S(1)} collective-permute-done((bf16[2,256,128]{2,1,0:T(8,128)(2,1)}, bf16[2,256,128]{2,1,0:T(8,128)(2,1)S(1)}, u32[]{:S(2)}, u32[]{:S(2)}) %collective-permute-start.4) | collective-permute-done | bytes 131104 | tf_op jit(solution)/shard_map/ppermute | solution.py:335
  64.2 4.4 %collective-permute-done.5.refs_6_ = bf16[2,256,128]{2,1,0:T(8,128)(2,1)S(1)} collective-permute-done((bf16[2,256,128]{2,1,0:T(8,128)(2,1)}, bf16[2,256,128]{2,1,0:T(8,128)(2,1)S(1)}, u32[]{:S(2)}, u32[]{:S(2)}) %collective-permute-start.5) | collective-permute-done | bytes 131104 | tf_op jit(solution)/shard_map/ppermute | solution.py:335
  68.7 1.5 %collective-permute-done.6.refs_7_ = bf16[2,256,128]{2,1,0:T(8,128)(2,1)S(1)} collective-permute-done((bf16[2,256,128]{2,1,0:T(8,128)(2,1)}, bf16[2,256,128]{2,1,0:T(8,128)(2,1)S(1)}, u32[]{:S(2)}, u32[]{:S(2)}) %collective-permute-start.6) | collective-permute-done | bytes 131104 | tf_op jit(solution)/shard_map/ppermute | solution.py:335
  70.2 0.5 collective-permute-start.12
  70.7 2.3 %collective-permute-done.1.refs_2_ = bf16[2,256,128]{2,1,0:T(8,128)(2,1)S(1)} collective-permute-done((bf16[2,256,128]{2,1,0:T(8,128)(2,1)}, bf16[2,256,128]{2,1,0:T(8,128)(2,1)S(1)}, u32[]{:S(2)}, u32[]{:S(2)}) %collective-permute-start.1) | collective-permute-done | bytes 131104 | tf_op jit(solution)/shard_map/ppermute | solution.py:335
  73.0 0.5 collective-permute-start.14
  73.6 0.4 collective-permute-start.9
  74.0 0.3 collective-permute-done.13.refs_14_
  74.5 0.3 collective-permute-done.8.refs_9_
  74.8 0.3 collective-permute-done.9.refs_10_
  75.2 0.3 copy-done.21
  75.5 0.3 copy-done.22
  75.8 0.7 copy-done.7
  76.6 6.8 %far.1 = bf16[32,80,128]{2,1,0:T(8,128)(2,1)} custom-call(bf16[2048,128]{1,0:T(8,128)(2,1)} %bitcast.3, bf16[2,256,128]{2,1,0:T(8,128)(2,1)} %get-tuple-element.18.refs_0_, bf16[2,256,128]{2,1,0:T(8,128)(2,1)} %copy-done.13, bf16[2,256,128]{2,1,0:T(8,128)(2,1)} %copy-done.14, bf16[2,256,128]{2,1,0:T(8,128)(2,1)} %copy-done.8, ...), custom_call_target="tpu_custom_call" | custom-call | tf_op jit(solution)/shard_map/far/pallas_call | solution.py:367
  83.4 12.3 %all-to-all-start.1 = ((bf16[32,80,128]{2,1,0:T(8,128)(2,1)}), bf16[32,80,128]{2,1,0:T(8,128)(2,1)S(1)}, u32[]{:S(2)}, u32[]{:S(2)}) async-start(bf16[32,80,128]{2,1,0:T(8,128)(2,1)} %far.1), calls=%async_computation.1 | async-start | bytes 1310720 | tf_op jit(solution)/shard_map/all_to_all | solution.py:384
  95.7 0.5 collective-permute-start.15
  96.2 2.2 %collective-permute-start.16 = (bf16[16,128]{1,0:T(8,128)(2,1)S(1)}, bf16[16,128]{1,0:T(8,128)(2,1)S(1)}, u32[]{:S(2)}, u32[]{:S(2)}) collective-permute-start(bf16[16,128]{1,0:T(8,128)(2,1)S(1)} %copy-done.5), channel_id=1, source_target_pairs={{0,4},{2,6},{4,0},{6,2},{1,5},{3,7},{5,1},{7,3},{8,12},{10,14},{12... | collective-permute-start | bytes 12296 | tf_op jit(solution)/shard_map/ppermute | solution.py:339
  98.4 2.1 %collective-permute-start.17 = (bf16[16,128]{1,0:T(8,128)(2,1)S(1)}, bf16[16,128]{1,0:T(8,128)(2,1)S(1)}, u32[]{:S(2)}, u32[]{:S(2)}) collective-permute-start(bf16[16,128]{1,0:T(8,128)(2,1)S(1)} %copy-done.5), channel_id=1, source_target_pairs={{0,6},{2,4},{4,2},{6,0},{1,7},{3,5},{5,3},{7,1},{8,14},{10,12},{12... | collective-permute-start | bytes 12296 | tf_op jit(solution)/shard_map/ppermute | solution.py:339
  100.6 1.6 %copy-done.1 = bf16[8,256,512]{2,1,0:T(8,128)(2,1)S(1)} copy-done((bf16[8,256,512]{2,1,0:T(8,128)(2,1)S(1)}, bf16[8,256,512]{2,1,0:T(8,128)(2,1)}, u32[]{:S(2)}) %copy-start.1) | copy-done | bytes 2097176
  102.1 4.0 %near.1 = (f32[32,8,128]{2,1,0:T(8,128)S(1)}, f32[32,8,128]{2,1,0:T(8,128)S(1)}) custom-call(s32[8]{0:T(128)S(1)} %copy-done.6, bf16[8,4096]{1,0:T(8,128)(2,1)S(1)} %copy-done.2, bf16[8,512]{1,0:T(8,128)(2,1)S(1)} %copy-done.3, bf16[8,512]{1,0:T(8,128)(2,1)S(1)} %copy-done.4, bf16[8,256,512]{2,1,0:T(8,128)(2,1)S(1)} %copy-done, ...), custom_call_target="tpu_custom_call" | custom-call | flops 300000000 | bytes 4500000 | tf_op jit(solution)/shard_map/near/pallas_call | solution.py:341
  106.2 11.1 %all-to-all-done.1.back_ref = bf16[32,80,128]{2,1,0:T(8,128)(2,1)S(1)} async-done(((bf16[32,80,128]{2,1,0:T(8,128)(2,1)}), bf16[32,80,128]{2,1,0:T(8,128)(2,1)S(1)}, u32[]{:S(2)}, u32[]{:S(2)}) %all-to-all-start.1) | async-done | bytes 655392 | tf_op jit(solution)/shard_map/all_to_all | solution.py:384
  117.3 0.5 select.1
  117.8 8.1 %all_to_all.15.back_ref = bf16[4,80,128]{2,1,0:T(8,128)(2,1)S(1)} all-to-all(bf16[4,80,128]{2,1,0:T(8,128)(2,1)S(1)} %select.1), channel_id=1, replica_groups=mesh['xh'=2,'z'=8,'xl'=2,'y'=4,'c'=2] {'y'}, dimensions={0} | all-to-all | bytes 163840 | tf_op jit(solution)/shard_map/all_to_all | solution.py:393
  125.9 0.8 merge.1
  (60 shorter events, 0.7 us)
Async XLA Ops:
  33.8 41.3 %all-to-all-start = ((bf16[128,16,128]{2,1,0:T(8,128)(2,1)}), bf16[128,16,128]{2,1,0:T(8,128)(2,1)S(1)}, u32[]{:S(2)}, u32[]{:S(2)}) async-start(bf16[128,16,128]{2,1,0:T(8,128)(2,1)} %bitcast.4), calls=%async_computation | async-start | bytes 1048576 | tf_op jit(solution)/shard_map/all_to_all | solution.py:332
  48.9 9.8 %collective-permute-start.2 = (bf16[2,256,128]{2,1,0:T(8,128)(2,1)}, bf16[2,256,128]{2,1,0:T(8,128)(2,1)S(1)}, u32[]{:S(2)}, u32[]{:S(2)}) collective-permute-start(bf16[2,256,128]{2,1,0:T(8,128)(2,1)} %get-tuple-element.21), channel_id=1, source_target_pairs={{0,6},{2,4},{4,2},{6,0},{8,14},{10,12},{12,10},{14,8},{1,7},{3,5},... | collective-permute-start | bytes 393224 | tf_op jit(solution)/shard_map/ppermute | solution.py:335
  51.6 8.6 %collective-permute-start.3 = (bf16[2,256,128]{2,1,0:T(8,128)(2,1)}, bf16[2,256,128]{2,1,0:T(8,128)(2,1)S(1)}, u32[]{:S(2)}, u32[]{:S(2)}) collective-permute-start(bf16[2,256,128]{2,1,0:T(8,128)(2,1)} %get-tuple-element.22), channel_id=1, source_target_pairs={{0,8},{2,10},{4,12},{6,14},{8,0},{10,2},{12,4},{14,6},{1,9},{3,11}... | collective-permute-start | bytes 393224 | tf_op jit(solution)/shard_map/ppermute | solution.py:335
  53.1 11.1 %collective-permute-start.4 = (bf16[2,256,128]{2,1,0:T(8,128)(2,1)}, bf16[2,256,128]{2,1,0:T(8,128)(2,1)S(1)}, u32[]{:S(2)}, u32[]{:S(2)}) collective-permute-start(bf16[2,256,128]{2,1,0:T(8,128)(2,1)} %get-tuple-element.23), channel_id=1, source_target_pairs={{0,10},{2,8},{4,14},{6,12},{8,2},{10,0},{12,6},{14,4},{1,11},{3,9}... | collective-permute-start | bytes 393224 | tf_op jit(solution)/shard_map/ppermute | solution.py:335
  53.3 15.3 %collective-permute-start.5 = (bf16[2,256,128]{2,1,0:T(8,128)(2,1)}, bf16[2,256,128]{2,1,0:T(8,128)(2,1)S(1)}, u32[]{:S(2)}, u32[]{:S(2)}) collective-permute-start(bf16[2,256,128]{2,1,0:T(8,128)(2,1)} %get-tuple-element.24), channel_id=1, source_target_pairs={{0,12},{2,14},{4,8},{6,10},{8,4},{10,6},{12,0},{14,2},{1,13},{3,15... | collective-permute-start | bytes 393224 | tf_op jit(solution)/shard_map/ppermute | solution.py:335
  56.0 14.2 %collective-permute-start.6 = (bf16[2,256,128]{2,1,0:T(8,128)(2,1)}, bf16[2,256,128]{2,1,0:T(8,128)(2,1)S(1)}, u32[]{:S(2)}, u32[]{:S(2)}) collective-permute-start(bf16[2,256,128]{2,1,0:T(8,128)(2,1)} %get-tuple-element.25), channel_id=1, source_target_pairs={{0,14},{2,12},{4,10},{6,8},{8,6},{10,4},{12,2},{14,0},{1,15},{3,13... | collective-permute-start | bytes 393224 | tf_op jit(solution)/shard_map/ppermute | solution.py:335
  58.7 17.1 %copy-start.8 = (bf16[2,256,128]{2,1,0:T(8,128)(2,1)}, bf16[2,256,128]{2,1,0:T(8,128)(2,1)S(1)}, u32[]{:S(2)}) copy-start(bf16[2,256,128]{2,1,0:T(8,128)(2,1)S(1)} %collective-permute-done.2.refs_3_) | copy-start | bytes 393220
  58.7 11.5 %collective-permute-start = (bf16[2,256,128]{2,1,0:T(8,128)(2,1)}, bf16[2,256,128]{2,1,0:T(8,128)(2,1)S(1)}, u32[]{:S(2)}, u32[]{:S(2)}) collective-permute-start(bf16[2,256,128]{2,1,0:T(8,128)(2,1)} %get-tuple-element.19), channel_id=1, source_target_pairs={{0,2},{2,0},{4,6},{6,4},{8,10},{10,8},{12,14},{14,12},{1,3},{3,1},... | collective-permute-start | bytes 393224 | tf_op jit(solution)/shard_map/ppermute | solution.py:335
  60.2 15.6 %copy-start.9 = (bf16[2,256,128]{2,1,0:T(8,128)(2,1)}, bf16[2,256,128]{2,1,0:T(8,128)(2,1)S(1)}, u32[]{:S(2)}) copy-start(bf16[2,256,128]{2,1,0:T(8,128)(2,1)S(1)} %collective-permute-done.3.refs_4_) | copy-start | bytes 393220
  60.2 12.7 %collective-permute-start.1 = (bf16[2,256,128]{2,1,0:T(8,128)(2,1)}, bf16[2,256,128]{2,1,0:T(8,128)(2,1)S(1)}, u32[]{:S(2)}, u32[]{:S(2)}) collective-permute-start(bf16[2,256,128]{2,1,0:T(8,128)(2,1)} %get-tuple-element.20), channel_id=1, source_target_pairs={{0,4},{2,6},{4,0},{6,2},{8,12},{10,14},{12,8},{14,10},{1,5},{3,7},... | collective-permute-start | bytes 393224 | tf_op jit(solution)/shard_map/ppermute | solution.py:335
  64.2 11.6 %copy-start.10 = (bf16[2,256,128]{2,1,0:T(8,128)(2,1)}, bf16[2,256,128]{2,1,0:T(8,128)(2,1)S(1)}, u32[]{:S(2)}) copy-start(bf16[2,256,128]{2,1,0:T(8,128)(2,1)S(1)} %collective-permute-done.4.refs_5_) | copy-start | bytes 393220
  64.2 8.8 %collective-permute-start.7 = (bf16[2,256,128]{2,1,0:T(8,128)(2,1)}, bf16[2,256,128]{2,1,0:T(8,128)(2,1)S(1)}, u32[]{:S(2)}, u32[]{:S(2)}) collective-permute-start(bf16[2,256,128]{2,1,0:T(8,128)(2,1)} %get-tuple-element.18.refs_0_), channel_id=1, source_target_pairs={{0,1},{1,0},{2,3},{3,2},{4,5},{5,4},{6,7},{7,6},{8,9},{9,8},{10,11... | collective-permute-start | bytes 393224 | tf_op jit(solution)/shard_map/ppermute | solution.py:336
  68.7 7.1 %copy-start.11 = (bf16[2,256,128]{2,1,0:T(8,128)(2,1)}, bf16[2,256,128]{2,1,0:T(8,128)(2,1)S(1)}, u32[]{:S(2)}) copy-start(bf16[2,256,128]{2,1,0:T(8,128)(2,1)S(1)} %collective-permute-done.5.refs_6_) | copy-start | bytes 393220
  68.7 4.8 %collective-permute-start.10 = (bf16[2,256,128]{2,1,0:T(8,128)(2,1)S(1)}, bf16[2,256,128]{2,1,0:T(8,128)(2,1)S(1)}, u32[]{:S(2)}, u32[]{:S(2)}) collective-permute-start(bf16[2,256,128]{2,1,0:T(8,128)(2,1)S(1)} %collective-permute-done.2.refs_3_), channel_id=1, source_target_pairs={{0,1},{1,0},{2,3},{3,2},{4,5},{5,4},{6,7},{7,6},{8,9},{9,8},{10,11... | collective-permute-start | bytes 393224 | tf_op jit(solution)/shard_map/ppermute | solution.py:336
  70.2 5.6 %copy-start.12 = (bf16[2,256,128]{2,1,0:T(8,128)(2,1)}, bf16[2,256,128]{2,1,0:T(8,128)(2,1)S(1)}, u32[]{:S(2)}) copy-start(bf16[2,256,128]{2,1,0:T(8,128)(2,1)S(1)} %collective-permute-done.6.refs_7_) | copy-start | bytes 393220
  70.2 3.4 %collective-permute-start.11 = (bf16[2,256,128]{2,1,0:T(8,128)(2,1)S(1)}, bf16[2,256,128]{2,1,0:T(8,128)(2,1)S(1)}, u32[]{:S(2)}, u32[]{:S(2)}) collective-permute-start(bf16[2,256,128]{2,1,0:T(8,128)(2,1)S(1)} %collective-permute-done.3.refs_4_), channel_id=1, source_target_pairs={{0,1},{1,0},{2,3},{3,2},{4,5},{5,4},{6,7},{7,6},{8,9},{9,8},{10,11... | collective-permute-start | bytes 393224 | tf_op jit(solution)/shard_map/ppermute | solution.py:336
  70.2 5.6 %copy-start.13 = (bf16[2,256,128]{2,1,0:T(8,128)(2,1)}, bf16[2,256,128]{2,1,0:T(8,128)(2,1)S(1)}, u32[]{:S(2)}) copy-start(bf16[2,256,128]{2,1,0:T(8,128)(2,1)S(1)} %collective-permute-done.refs_1_) | copy-start | bytes 393220
  70.2 3.8 %collective-permute-start.12 = (bf16[2,256,128]{2,1,0:T(8,128)(2,1)S(1)}, bf16[2,256,128]{2,1,0:T(8,128)(2,1)S(1)}, u32[]{:S(2)}, u32[]{:S(2)}) collective-permute-start(bf16[2,256,128]{2,1,0:T(8,128)(2,1)S(1)} %collective-permute-done.4.refs_5_), channel_id=1, source_target_pairs={{0,1},{1,0},{2,3},{3,2},{4,5},{5,4},{6,7},{7,6},{8,9},{9,8},{10,11... | collective-permute-start | bytes 393224 | tf_op jit(solution)/shard_map/ppermute | solution.py:336
  73.0 1.3 %collective-permute-start.13 = (bf16[2,256,128]{2,1,0:T(8,128)(2,1)S(1)}, bf16[2,256,128]{2,1,0:T(8,128)(2,1)S(1)}, u32[]{:S(2)}, u32[]{:S(2)}) collective-permute-start(bf16[2,256,128]{2,1,0:T(8,128)(2,1)S(1)} %collective-permute-done.5.refs_6_), channel_id=1, source_target_pairs={{0,1},{1,0},{2,3},{3,2},{4,5},{5,4},{6,7},{7,6},{8,9},{9,8},{10,11... | collective-permute-start | bytes 393224 | tf_op jit(solution)/shard_map/ppermute | solution.py:336
  73.0 1.5 %collective-permute-start.14 = (bf16[2,256,128]{2,1,0:T(8,128)(2,1)S(1)}, bf16[2,256,128]{2,1,0:T(8,128)(2,1)S(1)}, u32[]{:S(2)}, u32[]{:S(2)}) collective-permute-start(bf16[2,256,128]{2,1,0:T(8,128)(2,1)S(1)} %collective-permute-done.6.refs_7_), channel_id=1, source_target_pairs={{0,1},{1,0},{2,3},{3,2},{4,5},{5,4},{6,7},{7,6},{8,9},{9,8},{10,11... | collective-permute-start | bytes 393224 | tf_op jit(solution)/shard_map/ppermute | solution.py:336
  73.5 1.3 %collective-permute-start.8 = (bf16[2,256,128]{2,1,0:T(8,128)(2,1)S(1)}, bf16[2,256,128]{2,1,0:T(8,128)(2,1)S(1)}, u32[]{:S(2)}, u32[]{:S(2)}) collective-permute-start(bf16[2,256,128]{2,1,0:T(8,128)(2,1)S(1)} %collective-permute-done.refs_1_), channel_id=1, source_target_pairs={{0,1},{1,0},{2,3},{3,2},{4,5},{5,4},{6,7},{7,6},{8,9},{9,8},{10,11... | collective-permute-start | bytes 393224 | tf_op jit(solution)/shard_map/ppermute | solution.py:336
  73.6 1.5 %collective-permute-start.9 = (bf16[2,256,128]{2,1,0:T(8,128)(2,1)S(1)}, bf16[2,256,128]{2,1,0:T(8,128)(2,1)S(1)}, u32[]{:S(2)}, u32[]{:S(2)}) collective-permute-start(bf16[2,256,128]{2,1,0:T(8,128)(2,1)S(1)} %collective-permute-done.1.refs_2_), channel_id=1, source_target_pairs={{0,1},{1,0},{2,3},{3,2},{4,5},{5,4},{6,7},{7,6},{8,9},{9,8},{10,11... | collective-permute-start | bytes 393224 | tf_op jit(solution)/shard_map/ppermute | solution.py:336
  76.6 19.2 %copy-start.5 = (bf16[16,128]{1,0:T(8,128)(2,1)S(1)}, bf16[16,128]{1,0:T(8,128)(2,1)}, u32[]{:S(2)}) copy-start(bf16[16,128]{1,0:T(8,128)(2,1)} %get-tuple-element.26.refs_0_) | copy-start | bytes 12292
  76.6 23.9 %copy-start = (bf16[8,256,512]{2,1,0:T(8,128)(2,1)S(1)}, bf16[8,256,512]{2,1,0:T(8,128)(2,1)}, u32[]{:S(2)}) copy-start(bf16[8,256,512]{2,1,0:T(8,128)(2,1)} %key_ref.3) | copy-start | bytes 6291460
  76.6 23.9 %copy-start.2 = (bf16[8,4096]{1,0:T(8,128)(2,1)S(1)}, bf16[8,4096]{1,0:T(8,128)(2,1)}, u32[]{:S(2)}) copy-start(bf16[8,4096]{1,0:T(8,128)(2,1)} %query_ref.1) | copy-start | bytes 196612
  76.6 23.9 %copy-start.3 = (bf16[8,512]{1,0:T(8,128)(2,1)S(1)}, bf16[8,512]{1,0:T(8,128)(2,1)}, u32[]{:S(2)}) copy-start(bf16[8,512]{1,0:T(8,128)(2,1)} %new_key_ref.1) | copy-start | bytes 24580
  76.6 23.9 %copy-start.4 = (bf16[8,512]{1,0:T(8,128)(2,1)S(1)}, bf16[8,512]{1,0:T(8,128)(2,1)}, u32[]{:S(2)}) copy-start(bf16[8,512]{1,0:T(8,128)(2,1)} %new_value_ref.1) | copy-start | bytes 24580
  76.6 23.9 %copy-start.6 = (s32[8]{0:T(128)S(1)}, s32[8]{0:T(128)}, u32[]{:S(2)}) copy-start(s32[8]{0:T(128)} %len_ref.1) | copy-start | bytes 100
  83.4 33.9 %all-to-all-start.1 = ((bf16[32,80,128]{2,1,0:T(8,128)(2,1)}), bf16[32,80,128]{2,1,0:T(8,128)(2,1)S(1)}, u32[]{:S(2)}, u32[]{:S(2)}) async-start(bf16[32,80,128]{2,1,0:T(8,128)(2,1)} %far.1), calls=%async_computation.1 | async-start | bytes 1310720 | tf_op jit(solution)/shard_map/all_to_all | solution.py:384
  95.7 10.4 %collective-permute-start.15 = (bf16[16,128]{1,0:T(8,128)(2,1)S(1)}, bf16[16,128]{1,0:T(8,128)(2,1)S(1)}, u32[]{:S(2)}, u32[]{:S(2)}) collective-permute-start(bf16[16,128]{1,0:T(8,128)(2,1)S(1)} %copy-done.5), channel_id=1, source_target_pairs={{0,2},{2,0},{4,6},{6,4},{1,3},{3,1},{5,7},{7,5},{8,10},{10,8},{12,... | collective-permute-start | bytes 12296 | tf_op jit(solution)/shard_map/ppermute | solution.py:339
  96.2 9.9 %collective-permute-start.16 = (bf16[16,128]{1,0:T(8,128)(2,1)S(1)}, bf16[16,128]{1,0:T(8,128)(2,1)S(1)}, u32[]{:S(2)}, u32[]{:S(2)}) collective-permute-start(bf16[16,128]{1,0:T(8,128)(2,1)S(1)} %copy-done.5), channel_id=1, source_target_pairs={{0,4},{2,6},{4,0},{6,2},{1,5},{3,7},{5,1},{7,3},{8,12},{10,14},{12... | collective-permute-start | bytes 12296 | tf_op jit(solution)/shard_map/ppermute | solution.py:339
  98.4 7.8 %collective-permute-start.17 = (bf16[16,128]{1,0:T(8,128)(2,1)S(1)}, bf16[16,128]{1,0:T(8,128)(2,1)S(1)}, u32[]{:S(2)}, u32[]{:S(2)}) collective-permute-start(bf16[16,128]{1,0:T(8,128)(2,1)S(1)} %copy-done.5), channel_id=1, source_target_pairs={{0,6},{2,4},{4,2},{6,0},{1,7},{3,5},{5,3},{7,1},{8,14},{10,12},{12... | collective-permute-start | bytes 12296 | tf_op jit(solution)/shard_map/ppermute | solution.py:339
  (11 other events, 14.0 us)
